TPU v7x, 32 devices: a whole 2x2x4 slice. The times are simulated.
32 devices in a mesh: slab: 4 (over y, x), work: 8 (over z, core).
Axes of the slice: x: 2, y: 2, z: 4, core: 2. Of those that a mesh axis runs over, the one named last changes fastest.
Arguments:
- particles: float32 [8, 128, 128], P(None, ('slab', 'work')), may hold values from -5 to 5, as said below
- counts: int32 [128], P(('slab', 'work')), may hold values from 64 to 128
- partners: int32 [128, 8], P(('slab', 'work')), may hold values from 0 to 31
Outputs:
- density: float32 [128, 128], P(('slab', 'work'))
- acceleration: float32 [3, 128, 128], P(None, ('slab', 'work'))
Inputs may be any that keep to these rules, and one draw needn't show every extreme that they name: `particles`: rows 0 to 2 hold positions in [0, 1], rows 3 to 5 velocities in [-5, 5], row 6 smoothing lengths in [0.6, 1.2], row 7 masses in [0.0005, 0.004]. Slots from counts[g] on are empty. `partners`: partner bins lie in the bin's own slab.
All inputs are finite; a program needn't handle non-finite values.
Results may differ from a plain program's by a relative error of at most 0.00005.
Values sent between devices are 32-bit elements; how exact they have to be, the bound alone decides.
A program may use at most 64 MiB of HBM per device.

v0:
```python
import jax
import jax.numpy as jnp
from jax import lax
from jax.sharding import PartitionSpec as P

weight_norm = 21.0 / (16.0 * 3.141592653589793)
force_norm = 105.0 / (16.0 * 3.141592653589793)
viscosity = 0.25


def extended(shard, sides, width):
    for axis, dim in sides:
        count, length = (lax.axis_size(axis), shard.shape[dim])
        up = [(i, (i + 1) % count) for i in range(count)]
        down = [(j, i) for i, j in up]
        last = lax.slice_in_dim(shard, length - width, length, axis=dim)
        first = lax.slice_in_dim(shard, 0, width, axis=dim)
        before = lax.ppermute(last, axis, up)
        after = lax.ppermute(first, axis, down)
        shard = jnp.concatenate([before, shard, after], axis=dim)
    return shard


def separations(pos_self, pos_other):
    offset_vec = pos_self[:, :, None] - pos_other[:, None, :]
    radius = jnp.sqrt(jnp.sum(offset_vec * offset_vec, axis=0))
    return (offset_vec, radius)


def density_sum(pos_self, len_self, pos_other, mass_other):
    offset_vec, radius = separations(pos_self, pos_other)
    scaled = radius / len_self[:, None]
    shell_val = jnp.maximum(1.0 - 0.5 * scaled, 0.0)
    kernel = shell_val**4 * (1.0 + 2.0 * scaled) * (weight_norm / len_self**3)[:, None]
    return jnp.sum(kernel * mass_other[None, :], axis=1)


def force_sum(
    pos_self, vel_self, len_self, rho_self, pos_other, vel_other, len_other, mass_other, rho_other
):
    offset_vec, radius = separations(pos_self, pos_other)
    joint_h = 0.5 * (len_self[:, None] + len_other[None, :])
    scaled = radius / joint_h
    shell_val = jnp.maximum(1.0 - 0.5 * scaled, 0.0)
    factor = force_norm * shell_val**3 / joint_h**5 * mass_other[None, :]
    pressure = factor * (1.0 / rho_self[:, None] + 1.0 / rho_other[None, :])
    damping = factor * viscosity / (rho_self[:, None] * rho_other[None, :])
    veldiff = vel_self[:, :, None] - vel_other[:, None, :]
    return jnp.sum(pressure[None] * offset_vec - damping[None] * veldiff, axis=2)


def collect(link_ids, arrived):
    arrived_count = arrived.shape[1]
    offsets = jnp.arange(arrived_count, dtype=jnp.int32)
    chosen = (link_ids[:, None] == offsets[None, :]).astype(jnp.float32)
    return jnp.einsum("ln,cnp->clp", chosen, arrived, precision=lax.Precision.HIGHEST)


def density_bin(inputs):
    own_bin, gathered = inputs
    return density_sum(own_bin[0:3], own_bin[6], gathered[0:3], gathered[7])


def force_bin(inputs):
    own_bin, gathered = inputs
    return force_sum(
        own_bin[0:3],
        own_bin[3:6],
        own_bin[6],
        own_bin[8],
        gathered[0:3],
        gathered[3:6],
        gathered[6],
        gathered[7],
        gathered[8],
    )


def per_device(particles, counts, partners):
    channels, bin_count, slot_count = particles.shape
    link_count = partners.shape[1]
    slot_ids = jnp.arange(slot_count, dtype=jnp.int32)
    filled = (slot_ids[None, :] < counts[:, None]).astype(jnp.float32)
    masked = jnp.concatenate([particles[:7], particles[7:] * filled[None]], axis=0)
    link_ids = partners.reshape(-1)

    def gather_into(arrived):
        return collect(link_ids, arrived)

    def assemble(own_rows, rim_rows, far_rows, depth_rows):
        stacked = jnp.concatenate(
            [
                own_rows[:, :, None],
                rim_rows[0][:, :, None],
                rim_rows[2][:, :, None],
                far_rows.reshape(depth_rows, bin_count, link_count, slot_count),
            ],
            axis=2,
        )
        return jnp.transpose(stacked, (1, 0, 2, 3)).reshape(
            bin_count, depth_rows, (3 + link_count) * slot_count
        )

    rim_state = extended(masked[None], (("slab", 0),), 1)
    far_state = gather_into(lax.all_gather(masked, "work", axis=1, tiled=True))
    members = assemble(masked, rim_state, far_state, 8)
    owners = jnp.transpose(masked, (1, 0, 2))
    raw_density = lax.map(density_bin, (owners, members))
    safe_density = filled * raw_density + (1.0 - filled)
    density = filled * raw_density
    rim_rho = extended(safe_density[None, None], (("slab", 0),), 1)
    full_state = jnp.concatenate([masked, safe_density[None]], axis=0)
    far_rho = gather_into(lax.all_gather(safe_density[None], "work", axis=1, tiled=True))
    far_full = jnp.concatenate([far_state, far_rho], axis=0)
    rim_full = jnp.concatenate([rim_state, rim_rho], axis=1)
    members_full = assemble(full_state, rim_full, far_full, 9)
    owners_full = jnp.transpose(full_state, (1, 0, 2))
    acceleration = lax.map(force_bin, (owners_full, members_full)) * filled[:, None, :]
    return (density, jnp.transpose(acceleration, (1, 0, 2)))


def solution(mesh):
    placed = (P(None, ("slab", "work"), None), P(("slab", "work")), P(("slab", "work"), None))
    return jax.shard_map(
        per_device,
        mesh=mesh,
        in_specs=placed,
        out_specs=(P(("slab", "work"), None), P(None, ("slab", "work"), None)),
        check_vma=False,
    )
```

profile of v0, /device:TPU:0, one launch (start us, length us, event | category | flops | bytes accessed | tf_op | source)
XLA Modules:
  0.0 53.0 jit_solution(18294178015685573648)
XLA Ops:
  0.6 0.7 %slice.66 = f32[7,4,128]{2,1,0:T(4,128)S(1)} slice(f32[8,4,128]{2,1,0:T(4,128)} %param.7), slice={[0:7], [0:4], [0:128]} | slice | bytes 28672 | tf_op jit(solution)/shard_map/slice | solution.py:84
  1.3 0.7 %slice.67 = f32[1,4,128]{2,1,0:T(4,128)S(1)} slice(f32[8,4,128]{2,1,0:T(4,128)} %param.7), slice={[7:8], [0:4], [0:128]} | slice | bytes 4096 | tf_op jit(solution)/shard_map/slice | solution.py:84
  2.0 0.7 %compare_select_fusion = f32[1,4,128]{2,0,1:T(1,128)S(1)} fusion(f32[1,4,128]{2,0,1:T(1,128)S(1)} %bitcast.124, s32[4]{0:T(128)} %param.8), kind=kLoop, calls=%fused_computation.63 | loop fusion | flops 1024 | bytes 4112 | tf_op jit(solution)/shard_map/mul | solution.py:84
  2.8 3.0 %collective-permute-start = (f32[1,8,4,128]{3,1,2,0:T(8,128)S(1)}, f32[1,8,4,128]{3,1,2,0:T(8,128)S(1)}, u32[]{:S(2)}, u32[]{:S(2)}) collective-permute-start(f32[1,8,4,128]{3,1,2,0:T(8,128)S(1)} %fusion.31), channel_id=1, source_target_pairs={{0,8},{8,16},{16,24},{24,0},{1,9},{9,17},{17,25},{25,1},{2,10},{10... | collective-permute-start | bytes 49160 | tf_op jit(solution)/shard_map/ppermute | solution.py:18
  5.8 1.0 %collective-permute-start.1 = (f32[1,8,4,128]{3,1,2,0:T(8,128)S(1)}, f32[1,8,4,128]{3,1,2,0:T(8,128)S(1)}, u32[]{:S(2)}, u32[]{:S(2)}) collective-permute-start(f32[1,8,4,128]{3,1,2,0:T(8,128)S(1)} %fusion.31), channel_id=1, source_target_pairs={{8,0},{16,8},{24,16},{0,24},{9,1},{17,9},{25,17},{1,25},{10,2},{18... | collective-permute-start | bytes 49160 | tf_op jit(solution)/shard_map/ppermute | solution.py:19
  6.8 0.7 %fusion.24 = f32[4,128]{1,0:T(4,128)S(1)} fusion(s32[4]{0:T(128)} %param.8), kind=kLoop, calls=%fused_computation.67 | loop fusion | flops 1024 | bytes 2064 | tf_op jit(solution)/shard_map/convert_element_type | solution.py:83
  7.5 14.7 %all_gather.6 = f32[8,32,128]{2,0,1:T(8,128)S(1)} all-gather(f32[8,4,128]{2,0,1:T(8,128)S(1)} %pad_maximum_fusion.5), channel_id=1, replica_groups=mesh['slab'=4,'work'=8] {'work'}, dimensions={1}, use_global_device_ids=true | all-gather | bytes 147456 | tf_op jit(solution)/shard_map/all_gather | solution.py:105
  22.2 0.8 %eq.8 = s32[32]{0:T(128)S(1)} reshape(s32[4,8]{1,0:T(4,128)} %param.9) | data formatting | bytes 256 | tf_op jit(solution)/shard_map/eq | solution.py:55
  23.6 4.0 %while.22 = (s32[]{:T(128)}, f32[4,128]{1,0:T(4,128)S(1)}, f32[4,8,128]{2,1,0:T(8,128)S(1)}, f32[4,8,1408]{2,1,0:T(8,128)S(1)}) while((s32[]{:T(128)}, f32[4,128]{1,0:T(4,128)S(1)}, f32[4,8,128]{2,1,0:T(8,128)S(1)}, f32[4,8,1408]{2,1,0:T(8,128)S(1)}) %tuple.81), condition=%wide.region_3.4_spmd.clone, body=%wide.region_0.3_spmd.sunk.clone | while | flops 3604739 | bytes 1526869 | solution.py:108
  23.6 0.3 multiply_reduce_fusion.6
  24.0 0.6 %multiply_reduce_fusion.7 = f32[128]{0:T(128)S(1)} fusion(f32[128,1408]{1,0:T(8,128)S(1)} %multiply_reduce_fusion.6, f32[1408]{0:T(1024)S(1)} %dynamic-slice_reduce_fusion.3, f32[128]{0:T(128)S(1)} %fusion.45, f32[128]{0:T(128)S(1)} %slice_bitcast_fusion.7), kind=kLoop, calls=%fused_computation.1.clone.1.clone | loop fusion | flops 2162560 | bytes 728064 | tf_op jit(solution)/shard_map/while/body/eval_jaxpr/reduce_sum | solution.py:35
  24.6 0.3 multiply_reduce_fusion.6
  25.0 0.6 %multiply_reduce_fusion.7 = f32[128]{0:T(128)S(1)} fusion(f32[128,1408]{1,0:T(8,128)S(1)} %multiply_reduce_fusion.6, f32[1408]{0:T(1024)S(1)} %dynamic-slice_reduce_fusion.3, f32[128]{0:T(128)S(1)} %fusion.45, f32[128]{0:T(128)S(1)} %slice_bitcast_fusion.7), kind=kLoop, calls=%fused_computation.1.clone.1.clone | loop fusion | flops 2162560 | bytes 728064 | tf_op jit(solution)/shard_map/while/body/eval_jaxpr/reduce_sum | solution.py:35
  25.6 0.3 multiply_reduce_fusion.6
  26.0 0.6 %multiply_reduce_fusion.7 = f32[128]{0:T(128)S(1)} fusion(f32[128,1408]{1,0:T(8,128)S(1)} %multiply_reduce_fusion.6, f32[1408]{0:T(1024)S(1)} %dynamic-slice_reduce_fusion.3, f32[128]{0:T(128)S(1)} %fusion.45, f32[128]{0:T(128)S(1)} %slice_bitcast_fusion.7), kind=kLoop, calls=%fused_computation.1.clone.1.clone | loop fusion | flops 2162560 | bytes 728064 | tf_op jit(solution)/shard_map/while/body/eval_jaxpr/reduce_sum | solution.py:35
  26.6 0.3 multiply_reduce_fusion.6
  26.9 0.6 %multiply_reduce_fusion.7 = f32[128]{0:T(128)S(1)} fusion(f32[128,1408]{1,0:T(8,128)S(1)} %multiply_reduce_fusion.6, f32[1408]{0:T(1024)S(1)} %dynamic-slice_reduce_fusion.3, f32[128]{0:T(128)S(1)} %fusion.45, f32[128]{0:T(128)S(1)} %slice_bitcast_fusion.7), kind=kLoop, calls=%fused_computation.1.clone.1.clone | loop fusion | flops 2162560 | bytes 728064 | tf_op jit(solution)/shard_map/while/body/eval_jaxpr/reduce_sum | solution.py:35
  27.5 0.6 %subtract_add_fusion = (f32[4,128]{1,0:T(4,128)S(1)}, f32[4,128]{1,0:T(4,128)}) fusion(s32[4]{0:T(128)S(1)} %copy-done, f32[4,128]{1,0:T(4,128)S(1)} %get-tuple-element.46), kind=kLoop, calls=%fused_computation.65 | loop fusion | flops 2560 | bytes 6160 | tf_op jit(solution)/shard_map/add | solution.py:109
  28.2 0.6 %collective-permute-start.2 = (f32[1,1,4,128]{3,1,2,0:T(1,128)S(1)}, f32[1,1,4,128]{3,1,2,0:T(1,128)S(1)}, u32[]{:S(2)}, u32[]{:S(2)}) collective-permute-start(f32[1,1,4,128]{3,1,2,0:T(1,128)S(1)} %bitcast.118), channel_id=1, source_target_pairs={{0,8},{8,16},{16,24},{24,0},{1,9},{9,17},{17,25},{25,1},{2,10},{10... | collective-permute-start | bytes 6152 | tf_op jit(solution)/shard_map/ppermute | solution.py:18
  28.8 2.3 %collective-permute-start.3 = (f32[1,1,4,128]{3,1,2,0:T(1,128)S(1)}, f32[1,1,4,128]{3,1,2,0:T(1,128)S(1)}, u32[]{:S(2)}, u32[]{:S(2)}) collective-permute-start(f32[1,1,4,128]{3,1,2,0:T(1,128)S(1)} %bitcast.119), channel_id=1, source_target_pairs={{8,0},{16,8},{24,16},{0,24},{9,1},{17,9},{25,17},{1,25},{10,2},{18... | collective-permute-start | bytes 6152 | tf_op jit(solution)/shard_map/ppermute | solution.py:19
  31.1 12.7 %all-gather.1 = f32[8,4,128]{2,1,0:T(4,128)S(1)} all-gather(f32[1,4,128]{2,1,0:T(4,128)S(1)} %bitcast.120), channel_id=2, replica_groups=mesh['slab'=4,'work'=8] {'work'}, dimensions={0}, use_global_device_ids=true | all-gather | bytes 18432 | tf_op jit(solution)/shard_map/all_gather | solution.py:113
  44.4 8.0 %while.23 = (s32[]{:T(128)}, f32[4,3,128]{2,0,1:T(4,128)S(1)}, f32[4,9,128]{2,1,0:T(8,128)S(1)}, f32[4,9,1408]{2,0,1:T(4,128)S(1)}) while((s32[]{:T(128)}, f32[4,3,128]{2,0,1:T(4,128)S(1)}, f32[4,9,128]{2,1,0:T(8,128)S(1)}, f32[4,9,1408]{2,0,1:T(4,128)S(1)}) %tuple.78), condition=%wide.region_7.8_spmd.clone, body=%wide.region_4.7_spmd.sunk.clone | while | flops 8111238 | bytes 6043289 | solution.py:118
  44.5 0.3 fusion.49
  44.9 0.6 %add_multiply_fusion.3 = (f32[128,1408]{1,0:T(8,128)S(1)}, f32[128,1408]{1,0:T(8,128)S(1)}) fusion(f32[1408]{0:T(1024)S(1)} %broadcast_divide_fusion.6, f32[128]{0:T(128)S(1)} %get-tuple-element.205, f32[1408]{0:T(1024)S(1)} %get-tuple-element.206, f32[1408]{0:T(1024)S(1)} %get-tuple-element.207, f32[128]{0:T(128)S(1)} %fusion.48, ...), kind=kLoop, calls=%fused_computation.20.clone.1.clone | loop fusion | flops 2883584 | bytes 2180608 | tf_op jit(solution)/shard_map/while/body/eval_jaxpr/mul | solution.py:46
  45.7 0.6 %fusion.50 = f32[3,128]{1,0:T(4,128)S(1)} fusion(f32[3,1408]{1,0:T(4,128)S(1)} %get-tuple-element.202, f32[3,128]{1,0:T(4,128)S(1)} %get-tuple-element.203, f32[128,1408]{1,0:T(8,128)S(1)} %multiply_divide_fusion.3, f32[128,1408]{1,0:T(8,128)S(1)} %get-tuple-element.212, f32[3,1408]{1,0:T(4,128)S(1)} %get-tuple-element.208, ...), kind=kLoop, calls=%fused_computation.14.clone.1.clone | loop fusion | flops 3243648 | bytes 1480192 | tf_op jit(solution)/shard_map/while/body/eval_jaxpr/reduce_sum | solution.py:49
  46.9 0.6 %add_multiply_fusion.3 = (f32[128,1408]{1,0:T(8,128)S(1)}, f32[128,1408]{1,0:T(8,128)S(1)}) fusion(f32[1408]{0:T(1024)S(1)} %broadcast_divide_fusion.6, f32[128]{0:T(128)S(1)} %get-tuple-element.205, f32[1408]{0:T(1024)S(1)} %get-tuple-element.206, f32[1408]{0:T(1024)S(1)} %get-tuple-element.207, f32[128]{0:T(128)S(1)} %fusion.48, ...), kind=kLoop, calls=%fused_computation.20.clone.1.clone | loop fusion | flops 2883584 | bytes 2180608 | tf_op jit(solution)/shard_map/while/body/eval_jaxpr/mul | solution.py:46
  47.7 0.6 %fusion.50 = f32[3,128]{1,0:T(4,128)S(1)} fusion(f32[3,1408]{1,0:T(4,128)S(1)} %get-tuple-element.202, f32[3,128]{1,0:T(4,128)S(1)} %get-tuple-element.203, f32[128,1408]{1,0:T(8,128)S(1)} %multiply_divide_fusion.3, f32[128,1408]{1,0:T(8,128)S(1)} %get-tuple-element.212, f32[3,1408]{1,0:T(4,128)S(1)} %get-tuple-element.208, ...), kind=kLoop, calls=%fused_computation.14.clone.1.clone | loop fusion | flops 3243648 | bytes 1480192 | tf_op jit(solution)/shard_map/while/body/eval_jaxpr/reduce_sum | solution.py:49
  48.9 0.6 %add_multiply_fusion.3 = (f32[128,1408]{1,0:T(8,128)S(1)}, f32[128,1408]{1,0:T(8,128)S(1)}) fusion(f32[1408]{0:T(1024)S(1)} %broadcast_divide_fusion.6, f32[128]{0:T(128)S(1)} %get-tuple-element.205, f32[1408]{0:T(1024)S(1)} %get-tuple-element.206, f32[1408]{0:T(1024)S(1)} %get-tuple-element.207, f32[128]{0:T(128)S(1)} %fusion.48, ...), kind=kLoop, calls=%fused_computation.20.clone.1.clone | loop fusion | flops 2883584 | bytes 2180608 | tf_op jit(solution)/shard_map/while/body/eval_jaxpr/mul | solution.py:46
  49.7 0.6 %fusion.50 = f32[3,128]{1,0:T(4,128)S(1)} fusion(f32[3,1408]{1,0:T(4,128)S(1)} %get-tuple-element.202, f32[3,128]{1,0:T(4,128)S(1)} %get-tuple-element.203, f32[128,1408]{1,0:T(8,128)S(1)} %multiply_divide_fusion.3, f32[128,1408]{1,0:T(8,128)S(1)} %get-tuple-element.212, f32[3,1408]{1,0:T(4,128)S(1)} %get-tuple-element.208, ...), kind=kLoop, calls=%fused_computation.14.clone.1.clone | loop fusion | flops 3243648 | bytes 1480192 | tf_op jit(solution)/shard_map/while/body/eval_jaxpr/reduce_sum | solution.py:49
  50.9 0.6 %add_multiply_fusion.3 = (f32[128,1408]{1,0:T(8,128)S(1)}, f32[128,1408]{1,0:T(8,128)S(1)}) fusion(f32[1408]{0:T(1024)S(1)} %broadcast_divide_fusion.6, f32[128]{0:T(128)S(1)} %get-tuple-element.205, f32[1408]{0:T(1024)S(1)} %get-tuple-element.206, f32[1408]{0:T(1024)S(1)} %get-tuple-element.207, f32[128]{0:T(128)S(1)} %fusion.48, ...), kind=kLoop, calls=%fused_computation.20.clone.1.clone | loop fusion | flops 2883584 | bytes 2180608 | tf_op jit(solution)/shard_map/while/body/eval_jaxpr/mul | solution.py:46
  51.7 0.6 %fusion.50 = f32[3,128]{1,0:T(4,128)S(1)} fusion(f32[3,1408]{1,0:T(4,128)S(1)} %get-tuple-element.202, f32[3,128]{1,0:T(4,128)S(1)} %get-tuple-element.203, f32[128,1408]{1,0:T(8,128)S(1)} %multiply_divide_fusion.3, f32[128,1408]{1,0:T(8,128)S(1)} %get-tuple-element.212, f32[3,1408]{1,0:T(4,128)S(1)} %get-tuple-element.208, ...), kind=kLoop, calls=%fused_computation.14.clone.1.clone | loop fusion | flops 3243648 | bytes 1480192 | tf_op jit(solution)/shard_map/while/body/eval_jaxpr/reduce_sum | solution.py:49
  52.4 0.6 %multiply_bitcast_fusion = f32[3,4,128]{2,1,0:T(4,128)} fusion(f32[4,3,128]{2,0,1:T(4,128)S(1)} %get-tuple-element.47, f32[4,128]{1,0:T(4,128)S(1)} %fusion.24), kind=kLoop, calls=%fused_computation.64 | loop fusion | flops 1536 | bytes 14336 | tf_op jit(solution)/shard_map/transpose | solution.py:119
  (99 shorter events, 3.7 us)
Async XLA Ops:
  2.8 20.5 %collective-permute-start = (f32[1,8,4,128]{3,1,2,0:T(8,128)S(1)}, f32[1,8,4,128]{3,1,2,0:T(8,128)S(1)}, u32[]{:S(2)}, u32[]{:S(2)}) collective-permute-start(f32[1,8,4,128]{3,1,2,0:T(8,128)S(1)} %fusion.31), channel_id=1, source_target_pairs={{0,8},{8,16},{16,24},{24,0},{1,9},{9,17},{17,25},{25,1},{2,10},{10... | collective-permute-start | bytes 49160 | tf_op jit(solution)/shard_map/ppermute | solution.py:18
  5.8 17.6 %collective-permute-start.1 = (f32[1,8,4,128]{3,1,2,0:T(8,128)S(1)}, f32[1,8,4,128]{3,1,2,0:T(8,128)S(1)}, u32[]{:S(2)}, u32[]{:S(2)}) collective-permute-start(f32[1,8,4,128]{3,1,2,0:T(8,128)S(1)} %fusion.31), channel_id=1, source_target_pairs={{8,0},{16,8},{24,16},{0,24},{9,1},{17,9},{25,17},{1,25},{10,2},{18... | collective-permute-start | bytes 49160 | tf_op jit(solution)/shard_map/ppermute | solution.py:19
  23.6 4.0 %copy-start = (s32[4]{0:T(128)S(1)}, s32[4]{0:T(128)}, u32[]{:S(2)}) copy-start(s32[4]{0:T(128)} %param.8) | copy-start | bytes 52
  28.2 15.9 %collective-permute-start.2 = (f32[1,1,4,128]{3,1,2,0:T(1,128)S(1)}, f32[1,1,4,128]{3,1,2,0:T(1,128)S(1)}, u32[]{:S(2)}, u32[]{:S(2)}) collective-permute-start(f32[1,1,4,128]{3,1,2,0:T(1,128)S(1)} %bitcast.118), channel_id=1, source_target_pairs={{0,8},{8,16},{16,24},{24,0},{1,9},{9,17},{17,25},{25,1},{2,10},{10... | collective-permute-start | bytes 6152 | tf_op jit(solution)/shard_map/ppermute | solution.py:18
  28.8 15.3 %collective-permute-start.3 = (f32[1,1,4,128]{3,1,2,0:T(1,128)S(1)}, f32[1,1,4,128]{3,1,2,0:T(1,128)S(1)}, u32[]{:S(2)}, u32[]{:S(2)}) collective-permute-start(f32[1,1,4,128]{3,1,2,0:T(1,128)S(1)} %bitcast.119), channel_id=1, source_target_pairs={{8,0},{16,8},{24,16},{0,24},{9,1},{17,9},{25,17},{1,25},{10,2},{18... | collective-permute-start | bytes 6152 | tf_op jit(solution)/shard_map/ppermute | solution.py:19
where the time goes:
time: 53.3 us; the launch traced here: 53 us
  blocking collectives  27.4 us (51%)
  other arithmetic  13.2 us (25%)
  starting transfers between devices  6.94 us (13%)
  local copies, waits for them, and re-layouts  3.58 us (7%)
  between operations  0.82 us (2%)
  loops' own time  0.59 us (1%)
    all_gather x1, blocking collectives, per_device(): far_state = gather_into(lax.all_gather(masked, 'work', axis=1, tiled=True))  14.7 us
    all_gather x1, blocking collectives, per_device(): lax.all_gather(safe_density[None], 'work', axis=1, tiled=True)  12.7 us
    ppermute x2, starting transfers between devices, extended(): before = lax.ppermute(last, axis, up)  3.59 us
    ppermute x2, starting transfers between devices, extended(): after = lax.ppermute(first, axis, down)  3.35 us
    mul x4, other arithmetic, force_sum(): pressure = factor * (1.0 / rho_self[:, None] + 1.0 / rho_other[None, :])  2.53 us
    reduce_sum x4, other arithmetic, force_sum(): jnp.sum(pressure[None] * offset_vec - damping[None] * veldiff, axis=2)  2.53 us
    reduce_sum x4, other arithmetic, density_sum(): return jnp.sum(kernel * mass_other[None, :], axis=1)  2.24 us
    reduce_sum x8, other arithmetic, separations(): radius = jnp.sqrt(jnp.sum(offset_vec * offset_vec, axis=0))  2.18 us
  transfers between devices with their start and end apart: 4, of which 0 were waited for; matrix products, arithmetic and copies ran while one was open for 4% of the time, Pallas kernels for 0%

commit v1 on v0

v1 whole, which is shorter than its diff:
```python
import functools

import jax
import jax.numpy as jnp
from jax import lax
from jax.experimental import pallas as pl
from jax.experimental.pallas import tpu as pltpu
from jax.sharding import PartitionSpec as P

weight_norm = 21.0 / (16.0 * 3.141592653589793)
force_norm = 105.0 / (16.0 * 3.141592653589793)
viscosity = 0.25

MESH = pl.DeviceIdType.MESH
F32 = jnp.float32
BF16 = jnp.bfloat16


def rounded(values):
    return values.astype(BF16).astype(F32)


def pieces(values):
    first = rounded(values)
    rest = values - first
    second = rounded(rest)
    return first, second, rest - second


def sub_iota(rows, slots):
    return lax.broadcasted_iota(jnp.int32, (rows, slots), 0)


def each(count, body):
    if count <= 16:
        for i in range(count):
            body(i)
    else:
        lax.fori_loop(0, count, lambda i, c: (body(i), c)[1], 0)


def kernel(
    n_slab,
    n_work,
    particles,
    counts,
    partners,
    density_out,
    accel_out,
    near,
    rest,
    invs,
    left_ops,
    h_wide,
    half_inv,
    right_ops,
    radius,
    force_hi,
    force_lo,
    sources,
    send_sem,
    recv_sem,
):
    nb, slots = particles.shape[1], particles.shape[2]
    links = partners.shape[1]
    members = 3 + links
    slab = lax.axis_index("slab")
    me = lax.axis_index("work")
    mine = me * nb
    slab_bins = n_work * nb
    up = lax.rem(slab + 1, n_slab)
    down = lax.rem(slab + n_slab - 1, n_slab)

    barrier = pltpu.get_barrier_semaphore()

    def greet(d):
        pl.semaphore_signal(
            barrier, 1, device_id={"work": lax.rem(me + d + 1, n_work)}, device_id_type=MESH
        )

    for other in (up, down):
        pl.semaphore_signal(barrier, 1, device_id={"slab": other}, device_id_type=MESH)
    each(n_work - 1, greet)

    lane = lax.broadcasted_iota(jnp.int32, (1, slots), 1)

    def filled_of(g):
        return (lane < counts[g]).astype(F32)

    for g in range(nb):
        state = particles[:, g, :]
        near[mine + g] = jnp.concatenate([state[0:3], state[7:8] * filled_of(g)], axis=0)
        rest[mine + g] = state[3:7]

    pl.semaphore_wait(barrier, n_work + 1)

    def send(buf, step):
        src = buf.at[pl.ds(mine, nb)]

        def start(dst, where):
            pltpu.make_async_remote_copy(
                src_ref=src,
                dst_ref=dst,
                send_sem=send_sem.at[step],
                recv_sem=recv_sem.at[step],
                device_id=where,
                device_id_type=MESH,
            ).start()

        each(n_work - 1, lambda d: start(src, {"work": lax.rem(me + d + 1, n_work)}))
        start(buf.at[pl.ds(slab_bins, nb)], {"slab": up})
        start(buf.at[pl.ds(slab_bins + nb, nb)], {"slab": down})

    def wait(buf, step, sem):
        block = buf.at[pl.ds(0, slab_bins + nb)]
        pltpu.make_async_copy(block, block, sem.at[step]).wait()

    send(near, 0)
    send(rest, 1)

    def member_index(g, k):
        if k == 0:
            return mine + g
        if k == 1:
            return slab_bins + g
        if k == 2:
            return slab_bins + nb + g
        return partners[g, k - 3]

    row4 = sub_iota(4, slots)
    row8 = sub_iota(8, slots)
    spare = jnp.zeros((8, slots), F32)

    def centre(g):
        return jnp.mean(particles[0:7, g, :], axis=1, keepdims=True)

    def offset(values, mid):
        shifted = jnp.where(row4 < 3, values - mid, 0.0)
        return shifted, jnp.sum(shifted * shifted, axis=0, keepdims=True)

    centres = []
    for g in range(nb):
        mid = centre(g)
        mid_pos = jnp.concatenate([mid[0:3], jnp.zeros((1, 1), F32)], axis=0)
        centres.append((mid_pos, mid[3:6]))
        shifted, length = offset(near[mine + g], mid_pos)
        own = jnp.where(row4 < 3, -2.0 * shifted, length)
        p0, p1, p2 = pieces(jnp.concatenate([own, own], axis=0))
        row = row8 % 4
        a0 = jnp.where(row < 3, p0, 1.0)
        left = jnp.concatenate(
            [
                a0,
                jnp.where(row8 < 4, a0, jnp.where(row < 3, p1, p0)),
                jnp.where(row8 < 4, p1, p2),
                spare,
            ],
            axis=0,
        )
        left_ops[g] = left.T.astype(BF16)
        h_row = particles[6, g : g + 1, :]
        h_wide[g] = jnp.broadcast_to(h_row, (slots, slots)).T
        half_inv[g] = jnp.broadcast_to(0.5 / h_row, (slots, slots)).T

    wait(near, 0, recv_sem)

    for g in range(nb):
        mid_pos, mid_vel = centres[g]
        for k in range(members):
            shifted, length = offset(near[member_index(g, k)], mid_pos)
            other = jnp.where(row4 < 3, shifted, length)
            q0, q1, q2 = pieces(jnp.concatenate([other, other], axis=0))
            row = row8 % 4
            one0 = jnp.where(row < 3, q0, 1.0)
            right = jnp.concatenate(
                [
                    jnp.where(row8 < 4, q0, q1),
                    jnp.where(row8 < 4, q2, one0),
                    jnp.where(row8 < 4, jnp.where(row < 3, q1, 1.0), one0),
                    spare,
                ],
                axis=0,
            )
            right_ops[g, :, k * slots : (k + 1) * slots] = right.astype(BF16)
        acc = jnp.zeros((slots, slots), F32)
        for k0 in range(0, members, 2):
            ks = range(k0, min(k0 + 2, members))
            square = jnp.dot(
                left_ops[g],
                right_ops[g, :, k0 * slots : (k0 + len(ks)) * slots],
                preferred_element_type=F32,
            )
            square = jnp.maximum(square, 1e-30)
            dist = square * lax.rsqrt(square)
            radius[g, :, k0 * slots : (k0 + len(ks)) * slots] = dist
            for k in ks:
                mass = near[member_index(g, k)][3:4]
                shell = jnp.maximum(
                    1.0 - dist[:, (k - k0) * slots : (k - k0 + 1) * slots] * half_inv[g], 0.0
                )
                shell2 = shell * shell
                acc += (shell2 * shell2) * ((1.25 - shell) * mass)
        total = jnp.sum(acc.T, axis=0, keepdims=True)
        filled = filled_of(g)
        h_row = particles[6, g : g + 1, :]
        raw = total * (4.0 * weight_norm / (h_row * h_row * h_row))
        density_out[g : g + 1, :] = filled * raw
        invs[mine + g] = 1.0 / (filled * raw + (1.0 - filled))

    send(invs, 2)
    wait(rest, 1, recv_sem)

    for g in range(nb):
        for k in range(members):
            cols = slice(k * slots, (k + 1) * slots)
            both = h_wide[g] + rest[member_index(g, k)][3:4]
            inv = 1.0 / both
            inv2 = inv * inv
            gap = jnp.maximum(both - radius[g, :, cols], 0.0)
            part = gap * inv2
            force = (part * part) * (part * inv2)
            high = force.astype(BF16)
            force_hi[g, :, cols] = high
            force_lo[g, :, cols] = (force - high.astype(F32)).astype(BF16)

    wait(invs, 2, recv_sem)

    for g in range(nb):
        mid_pos, mid_vel = centres[g]
        mid_four = jnp.concatenate([mid_vel, jnp.zeros((1, 1), F32)], axis=0)
        for k in range(members):
            at = member_index(g, k)
            place = near[at]
            mass = place[3:4]
            moment = jnp.where(row4 < 3, place - mid_pos, 1.0) * mass
            speed = (rest[at] - mid_four) * mass
            inv = invs[at]
            first = jnp.concatenate([moment, moment * inv], axis=0)
            second = jnp.where(row8 < 3, jnp.concatenate([speed, speed], axis=0) * inv, 0.0)
            b0, b1, b2 = pieces(jnp.concatenate([first, second], axis=0))
            sources[g, :, k * slots : (k + 1) * slots] = jnp.concatenate(
                [b0, b1, b2], axis=0
            ).astype(BF16)
        dims = (((1,), (1,)), ((), ()))
        sums = lax.dot_general(
            force_hi[g], sources[g], dims, preferred_element_type=F32
        ) + lax.dot_general(force_lo[g], sources[g], dims, preferred_element_type=F32)
        sums = sums.T
        sums = sums[0:16] + sums[16:32] + sums[32:48]
        own = particles[:, g, :]
        pos = own[0:3] - mid_pos[0:3]
        vel = own[3:6] - mid_vel
        inv = invs[mine + g]
        s1, s0, t1, t0, tv = sums[0:3], sums[3:4], sums[4:7], sums[7:8], sums[8:11]
        result = inv * (pos * s0 - s1) + (pos * t0 - t1) - (viscosity * inv) * (vel * t0 - tv)
        accel_out[:, g, :] = result * (filled_of(g) * (32.0 * force_norm))

    for step, buf in enumerate((near, rest, invs)):
        wait(buf, step, send_sem)


def per_device(n_slab, n_work, particles, counts, partners):
    channels, nb, slots = particles.shape
    members = 3 + partners.shape[1]
    bins = (n_work + 2) * nb
    vmem = pl.BlockSpec(memory_space=pltpu.VMEM)
    smem = pl.BlockSpec(memory_space=pltpu.SMEM)
    pairs = nb * members * slots * slots
    return pl.pallas_call(
        functools.partial(kernel, n_slab, n_work),
        out_shape=(
            jax.ShapeDtypeStruct((nb, slots), F32),
            jax.ShapeDtypeStruct((3, nb, slots), F32),
        ),
        in_specs=[vmem, smem, smem],
        out_specs=(vmem, vmem),
        scratch_shapes=[
            pltpu.VMEM((bins, 4, slots), F32),
            pltpu.VMEM((bins, 4, slots), F32),
            pltpu.VMEM((bins, 1, slots), F32),
            pltpu.VMEM((nb, slots, 32), BF16),
            pltpu.VMEM((nb, slots, slots), F32),
            pltpu.VMEM((nb, slots, slots), F32),
            pltpu.VMEM((nb, 32, members * slots), BF16),
            pltpu.VMEM((nb, slots, members * slots), F32),
            pltpu.VMEM((nb, slots, members * slots), BF16),
            pltpu.VMEM((nb, slots, members * slots), BF16),
            pltpu.VMEM((nb, 48, members * slots), BF16),
            pltpu.SemaphoreType.DMA((3,)),
            pltpu.SemaphoreType.DMA((3,)),
        ],
        compiler_params=pltpu.CompilerParams(
            collective_id=0, has_side_effects=True, vmem_limit_bytes=40 * 1024 * 1024
        ),
        cost_estimate=pl.CostEstimate(flops=40 * pairs, bytes_accessed=65536, transcendentals=0),
    )(particles, counts, partners)


def solution(mesh):
    placed = (P(None, ("slab", "work"), None), P(("slab", "work")), P(("slab", "work"), None))
    return jax.shard_map(
        functools.partial(per_device, mesh.shape["slab"], mesh.shape["work"]),
        mesh=mesh,
        in_specs=placed,
        out_specs=(P(("slab", "work"), None), P(None, ("slab", "work"), None)),
        check_vma=False,
    )
```

time: 53.3 us -> 20.4 us (0.38)
  blocking collectives: 27.4 us -> 0 us
  Pallas kernels: 0 us -> 16.2 us
  other arithmetic: 13.2 us -> 0 us
  starting transfers between devices: 6.94 us -> 0 us
  loops' own time: 0.59 us -> 0 us
    all_gather x2 -> x0, blocking collectives: 27.4 us -> none  [the longest x1 14.7 us: per_device(): far_state = gather_into(lax.all_gather(masked, 'work', axis=1, tiled=True))]
    pallas_call x0 -> x1, Pallas kernels: none -> 16.2 us  [per_device(): pl.pallas_call(functools.partial(kernel, n_slab, n_work), out_shape=(jax....]
    reduce_sum x16 -> x0, other arithmetic: 6.94 us -> none  [the longest x4 2.53 us: force_sum(): jnp.sum(pressure[None] * offset_vec - damping[None] * veldiff, axis=2)]
    ppermute x4 -> x0, starting transfers between devices: 6.94 us -> none  [the longest x2 3.59 us: extended(): before = lax.ppermute(last, axis, up)]
    mul x5 -> x0, other arithmetic: 3.26 us -> none  [the longest x4 2.53 us: force_sum(): pressure = factor * (1.0 / rho_self[:, None] + 1.0 / rho_other[None, :])]
    unnamed x3 -> x8, local copies, waits for them, and re-layouts: 0.01 us -> 3.22 us
    slice x14 -> x0, local copies, waits for them, and re-layouts: 1.91 us -> none  [the longest x1 0.72 us: per_device(): particles[:7]]
    transpose x4 -> x0, other arithmetic: 0.81 us -> none  [the longest x1 0.6 us: per_device(): return (density, jnp.transpose(acceleration, (1, 0, 2)))]
  transfers between devices with their start and end apart: 4 -> 0, of which waited for: 0 -> 0; matrix products, arithmetic and copies ran while one was open for 4% -> 0% of each run, Pallas kernels for 0% -> 0%
where the time goes in v1:
time: 20.4 us; the launch traced here: 20.1 us
  Pallas kernels  16.2 us (79%)
  local copies, waits for them, and re-layouts  3.22 us (16%)
  between operations  0.65 us (3%)
    pallas_call x1, Pallas kernels, per_device(): pl.pallas_call(functools.partial(kernel, n_slab, n_work), out_shape=(jax....  16.2 us
    unnamed x8, local copies, waits for them, and re-layouts  3.22 us

profile of v1, /device:TPU:0, one launch (start us, length us, event | category | flops | bytes accessed | tf_op | source)
XLA Modules:
  0.0 20.1 jit_solution(4577054954761999082)
XLA Ops:
  0.6 0.0 copy-start
  0.6 0.7 %copy-done = f32[8,4,128]{2,1,0:T(4,128)S(1)} copy-done((f32[8,4,128]{2,1,0:T(4,128)S(1)}, f32[8,4,128]{2,1,0:T(4,128)}, u32[]{:S(2)}) %copy-start) | copy-done | bytes 16408
  1.3 0.0 copy-start.1
  1.4 0.7 %copy-done.1 = s32[4,8]{1,0:T(4,128)S(1)} copy-done((s32[4,8]{1,0:T(4,128)S(1)}, s32[4,8]{1,0:T(4,128)}, u32[]{:S(2)}) %copy-start.1) | copy-done | bytes 152
  2.0 0.0 copy-start.2
  2.0 0.7 %copy-done.2 = s32[4]{0:T(128)S(1)} copy-done((s32[4]{0:T(128)S(1)}, s32[4]{0:T(128)}, u32[]{:S(2)}) %copy-start.2) | copy-done | bytes 40
  2.7 16.2 %shard_map.50 = (f32[4,128]{1,0:T(4,128)S(1)}, f32[3,4,128]{2,1,0:T(4,128)S(1)}) custom-call(f32[8,4,128]{2,1,0:T(4,128)S(1)} %copy-done, s32[4]{0:T(128)S(1)} %copy-done.2, s32[4,8]{1,0:T(4,128)S(1)} %copy-done.1), custom_call_target="tpu_custom_call" | custom-call | flops 28835840 | bytes 65536 | tf_op jit(solution)/shard_map/pallas_call | solution.py:269
  18.9 0.6 %copy.7 = f32[4,128]{1,0:T(4,128)} copy(f32[4,128]{1,0:T(4,128)S(1)} %get-tuple-element.4) | data formatting | bytes 4096
  19.5 0.6 %copy.8 = f32[3,4,128]{2,1,0:T(4,128)} copy(f32[3,4,128]{2,1,0:T(4,128)S(1)} %get-tuple-element.5) | data formatting | bytes 12288
Async XLA Ops:
  0.6 0.7 %copy-start = (f32[8,4,128]{2,1,0:T(4,128)S(1)}, f32[8,4,128]{2,1,0:T(4,128)}, u32[]{:S(2)}) copy-start(f32[8,4,128]{2,1,0:T(4,128)} %particles.1) | copy-start | bytes 49156
  1.3 0.7 %copy-start.1 = (s32[4,8]{1,0:T(4,128)S(1)}, s32[4,8]{1,0:T(4,128)}, u32[]{:S(2)}) copy-start(s32[4,8]{1,0:T(4,128)} %partners.1) | copy-start | bytes 388
  2.0 0.7 %copy-start.2 = (s32[4]{0:T(128)S(1)}, s32[4]{0:T(128)}, u32[]{:S(2)}) copy-start(s32[4]{0:T(128)} %counts.1) | copy-start | bytes 52

commit v2 on v1

--- a/solution.py
+++ b/solution.py
@@ -42,11 +42,14 @@
 def kernel(
     n_slab,
     n_work,
+    particles_in,
+    counts_in,
+    partners_in,
+    density_out,
+    accel_out,
     particles,
     counts,
     partners,
-    density_out,
-    accel_out,
     near,
     rest,
     invs,
@@ -60,6 +63,7 @@
     sources,
     send_sem,
     recv_sem,
+    read_sem,
 ):
     nb, slots = particles.shape[1], particles.shape[2]
     links = partners.shape[1]
@@ -71,6 +75,15 @@
     up = lax.rem(slab + 1, n_slab)
     down = lax.rem(slab + n_slab - 1, n_slab)
 
+    reads = [
+        pltpu.make_async_copy(src, dst, read_sem.at[i])
+        for i, (src, dst) in enumerate(
+            ((particles_in, particles), (counts_in, counts), (partners_in, partners))
+        )
+    ]
+    for read in reads:
+        read.start()
+
     barrier = pltpu.get_barrier_semaphore()
 
     def greet(d):
@@ -87,6 +100,8 @@
     def filled_of(g):
         return (lane < counts[g]).astype(F32)
 
+    for read in reads:
+        read.wait()
     for g in range(nb):
         state = particles[:, g, :]
         near[mine + g] = jnp.concatenate([state[0:3], state[7:8] * filled_of(g)], axis=0)
@@ -116,7 +131,6 @@
         pltpu.make_async_copy(block, block, sem.at[step]).wait()
 
     send(near, 0)
-    send(rest, 1)
 
     def member_index(g, k):
         if k == 0:
@@ -137,6 +151,23 @@
     def offset(values, mid):
         shifted = jnp.where(row4 < 3, values - mid, 0.0)
         return shifted, jnp.sum(shifted * shifted, axis=0, keepdims=True)
+
+    def build_right(g, k, mid_pos):
+        shifted, length = offset(near[member_index(g, k)], mid_pos)
+        other = jnp.where(row4 < 3, shifted, length)
+        q0, q1, q2 = pieces(jnp.concatenate([other, other], axis=0))
+        row = row8 % 4
+        one0 = jnp.where(row < 3, q0, 1.0)
+        right = jnp.concatenate(
+            [
+                jnp.where(row8 < 4, q0, q1),
+                jnp.where(row8 < 4, q2, one0),
+                jnp.where(row8 < 4, jnp.where(row < 3, q1, 1.0), one0),
+                spare,
+            ],
+            axis=0,
+        )
+        right_ops[g, :, k * slots : (k + 1) * slots] = right.astype(BF16)
 
     centres = []
     for g in range(nb):
@@ -158,30 +189,18 @@
             axis=0,
         )
         left_ops[g] = left.T.astype(BF16)
+        build_right(g, 0, mid_pos)
         h_row = particles[6, g : g + 1, :]
         h_wide[g] = jnp.broadcast_to(h_row, (slots, slots)).T
         half_inv[g] = jnp.broadcast_to(0.5 / h_row, (slots, slots)).T
 
     wait(near, 0, recv_sem)
+    send(rest, 1)
 
     for g in range(nb):
         mid_pos, mid_vel = centres[g]
-        for k in range(members):
-            shifted, length = offset(near[member_index(g, k)], mid_pos)
-            other = jnp.where(row4 < 3, shifted, length)
-            q0, q1, q2 = pieces(jnp.concatenate([other, other], axis=0))
-            row = row8 % 4
-            one0 = jnp.where(row < 3, q0, 1.0)
-            right = jnp.concatenate(
-                [
-                    jnp.where(row8 < 4, q0, q1),
-                    jnp.where(row8 < 4, q2, one0),
-                    jnp.where(row8 < 4, jnp.where(row < 3, q1, 1.0), one0),
-                    spare,
-                ],
-                axis=0,
-            )
-            right_ops[g, :, k * slots : (k + 1) * slots] = right.astype(BF16)
+        for k in range(1, members):
+            build_right(g, k, mid_pos)
         acc = jnp.zeros((slots, slots), F32)
         for k0 in range(0, members, 2):
             ks = range(k0, min(k0 + 2, members))
@@ -214,7 +233,7 @@
         for k in range(members):
             cols = slice(k * slots, (k + 1) * slots)
             both = h_wide[g] + rest[member_index(g, k)][3:4]
-            inv = 1.0 / both
+            inv = pltpu.reciprocal(both, approx=True)
             inv2 = inv * inv
             gap = jnp.maximum(both - radius[g, :, cols], 0.0)
             part = gap * inv2
@@ -264,7 +283,7 @@
     members = 3 + partners.shape[1]
     bins = (n_work + 2) * nb
     vmem = pl.BlockSpec(memory_space=pltpu.VMEM)
-    smem = pl.BlockSpec(memory_space=pltpu.SMEM)
+    hbm = pl.BlockSpec(memory_space=pltpu.HBM)
     pairs = nb * members * slots * slots
     return pl.pallas_call(
         functools.partial(kernel, n_slab, n_work),
@@ -272,9 +291,12 @@
             jax.ShapeDtypeStruct((nb, slots), F32),
             jax.ShapeDtypeStruct((3, nb, slots), F32),
         ),
-        in_specs=[vmem, smem, smem],
+        in_specs=[hbm, hbm, hbm],
         out_specs=(vmem, vmem),
         scratch_shapes=[
+            pltpu.VMEM(particles.shape, F32),
+            pltpu.SMEM(counts.shape, counts.dtype),
+            pltpu.SMEM(partners.shape, partners.dtype),
             pltpu.VMEM((bins, 4, slots), F32),
             pltpu.VMEM((bins, 4, slots), F32),
             pltpu.VMEM((bins, 1, slots), F32),
@@ -288,9 +310,10 @@
             pltpu.VMEM((nb, 48, members * slots), BF16),
             pltpu.SemaphoreType.DMA((3,)),
             pltpu.SemaphoreType.DMA((3,)),
+            pltpu.SemaphoreType.DMA((3,)),
         ],
         compiler_params=pltpu.CompilerParams(
-            collective_id=0, has_side_effects=True, vmem_limit_bytes=40 * 1024 * 1024
+            collective_id=0, has_side_effects=True, vmem_limit_bytes=64 * 1024 * 1024
         ),
         cost_estimate=pl.CostEstimate(flops=40 * pairs, bytes_accessed=65536, transcendentals=0),
     )(particles, counts, partners)

time: 20.4 us -> 18.7 us (0.917)
  local copies, waits for them, and re-layouts: 3.22 us -> 1.85 us
  Pallas kernels: 16.2 us -> 15.9 us
    unnamed x8 -> x4, local copies, waits for them, and re-layouts: 3.22 us -> 1.85 us
    pallas_call x1, Pallas kernels: 16.2 us -> 15.9 us  [per_device(): pl.pallas_call(functools.partial(kernel, n_slab, n_work), out_shape=(jax....]
where the time goes in v2:
time: 18.7 us; the launch traced here: 18.4 us
  Pallas kernels  15.9 us (85%)
  local copies, waits for them, and re-layouts  1.85 us (10%)
  between operations  0.65 us (3%)
    pallas_call x1, Pallas kernels, per_device(): pl.pallas_call(functools.partial(kernel, n_slab, n_work), out_shape=(jax....  15.9 us
    unnamed x4, local copies, waits for them, and re-layouts  1.85 us

profile of v2, /device:TPU:0, one launch (start us, length us, event | category | flops | bytes accessed | tf_op | source)
XLA Modules:
  0.0 18.4 jit_solution(778995339204983027)
XLA Ops:
  0.6 15.9 %shard_map.50 = (f32[4,128]{1,0:T(4,128)}, f32[3,4,128]{2,1,0:T(4,128)}) custom-call(f32[8,4,128]{2,1,0:T(4,128)} %particles_in.1, s32[4]{0:T(128)} %counts_in.1, s32[4,8]{1,0:T(4,128)} %partners_in.1), custom_call_target="tpu_custom_call" | custom-call | flops 28835840 | bytes 65536 | tf_op jit(solution)/shard_map/pallas_call | solution.py:288
  16.6 0.0 copy-start
  16.6 1.3 %copy.7 = f32[4,128]{1,0:T(4,128)} copy(f32[4,128]{1,0:T(4,128)} %get-tuple-element.4) | data formatting | bytes 4096
  17.8 0.0 copy-done
  17.8 0.6 %copy.8 = f32[3,4,128]{2,1,0:T(4,128)} copy(f32[3,4,128]{2,1,0:T(4,128)S(1)} %copy-done) | data formatting | bytes 12288
Async XLA Ops:
  16.6 1.3 %copy-start = (f32[3,4,128]{2,1,0:T(4,128)S(1)}, f32[3,4,128]{2,1,0:T(4,128)}, u32[]{:S(2)}) copy-start(f32[3,4,128]{2,1,0:T(4,128)} %get-tuple-element.5) | copy-start | bytes 18436

commit v3 on v2

--- a/solution.py
+++ b/solution.py
@@ -55,7 +55,8 @@
     invs,
     left_ops,
     h_wide,
-    half_inv,
+    reach,
+    limit,
     right_ops,
     radius,
     force_hi,
@@ -192,7 +193,8 @@
         build_right(g, 0, mid_pos)
         h_row = particles[6, g : g + 1, :]
         h_wide[g] = jnp.broadcast_to(h_row, (slots, slots)).T
-        half_inv[g] = jnp.broadcast_to(0.5 / h_row, (slots, slots)).T
+        reach[g] = 2.0 * h_wide[g]
+        limit[g] = 2.5 * h_wide[g]
 
     wait(near, 0, recv_sem)
     send(rest, 1)
@@ -214,15 +216,16 @@
             radius[g, :, k0 * slots : (k0 + len(ks)) * slots] = dist
             for k in ks:
                 mass = near[member_index(g, k)][3:4]
-                shell = jnp.maximum(
-                    1.0 - dist[:, (k - k0) * slots : (k - k0 + 1) * slots] * half_inv[g], 0.0
+                gap = jnp.maximum(
+                    reach[g] - dist[:, (k - k0) * slots : (k - k0 + 1) * slots], 0.0
                 )
-                shell2 = shell * shell
-                acc += (shell2 * shell2) * ((1.25 - shell) * mass)
+                gap2 = gap * gap
+                acc += (gap2 * gap2) * ((limit[g] - gap) * mass)
         total = jnp.sum(acc.T, axis=0, keepdims=True)
         filled = filled_of(g)
         h_row = particles[6, g : g + 1, :]
-        raw = total * (4.0 * weight_norm / (h_row * h_row * h_row))
+        h2 = h_row * h_row
+        raw = total * ((weight_norm / 8.0) / (h2 * h2 * h2 * h2))
         density_out[g : g + 1, :] = filled * raw
         invs[mine + g] = 1.0 / (filled * raw + (1.0 - filled))
 
@@ -303,6 +306,7 @@
             pltpu.VMEM((nb, slots, 32), BF16),
             pltpu.VMEM((nb, slots, slots), F32),
             pltpu.VMEM((nb, slots, slots), F32),
+            pltpu.VMEM((nb, slots, slots), F32),
             pltpu.VMEM((nb, 32, members * slots), BF16),
             pltpu.VMEM((nb, slots, members * slots), F32),
             pltpu.VMEM((nb, slots, members * slots), BF16),
@@ -313,10 +317,10 @@
             pltpu.SemaphoreType.DMA((3,)),
         ],
         compiler_params=pltpu.CompilerParams(
-            collective_id=0, has_side_effects=True, vmem_limit_bytes=64 * 1024 * 1024
+            collective_id=0, has_side_effects=True, vmem_limit_bytes=40 * 1024 * 1024
         ),
         cost_estimate=pl.CostEstimate(flops=40 * pairs, bytes_accessed=65536, transcendentals=0),
-    )(particles, counts, partners)
+    )(*(pltpu.with_memory_space_constraint(a, pltpu.HBM) for a in (particles, counts, partners)))
 
 
 def solution(mesh):

time: 18.7 us -> 17.4 us (0.930)
  local copies, waits for them, and re-layouts: 1.85 us -> 1.17 us
  Pallas kernels: 15.9 us -> 15.4 us
    unnamed x4 -> x2, local copies, waits for them, and re-layouts: 1.85 us -> 1.17 us
    pallas_call x1, Pallas kernels: 15.9 us -> 15.4 us  [per_device(): pl.pallas_call(functools.partial(kernel, n_slab, n_work), out_shape=(jax....]
where the time goes in v3:
time: 17.4 us; the launch traced here: 17.2 us
  Pallas kernels  15.4 us (89%)
  local copies, waits for them, and re-layouts  1.17 us (7%)
  between operations  0.64 us (4%)
    pallas_call x1, Pallas kernels, per_device(): pl.pallas_call(functools.partial(kernel, n_slab, n_work), out_shape=(jax....  15.4 us
    unnamed x2, local copies, waits for them, and re-layouts  1.17 us

profile of v3, /device:TPU:0, one launch (start us, length us, event | category | flops | bytes accessed | tf_op | source)
XLA Modules:
  0.0 17.2 jit_solution(3791383348417897030)
XLA Ops:
  0.6 15.4 %shard_map.50 = (f32[4,128]{1,0:T(4,128)S(1)}, f32[3,4,128]{2,1,0:T(4,128)S(1)}) custom-call(f32[8,4,128]{2,1,0:T(4,128)} %particles_in.1, s32[4]{0:T(128)} %counts_in.1, s32[4,8]{1,0:T(4,128)} %partners_in.1), custom_call_target="tpu_custom_call" | custom-call | flops 28835840 | bytes 65536 | tf_op jit(solution)/shard_map/pallas_call | solution.py:291
  16.0 0.6 %copy.7 = f32[4,128]{1,0:T(4,128)} copy(f32[4,128]{1,0:T(4,128)S(1)} %get-tuple-element.4) | data formatting | bytes 4096
  16.6 0.6 %copy.8 = f32[3,4,128]{2,1,0:T(4,128)} copy(f32[3,4,128]{2,1,0:T(4,128)S(1)} %get-tuple-element.5) | data formatting | bytes 12288

commit v4 on v3

--- a/solution.py
+++ b/solution.py
@@ -53,6 +53,7 @@
     near,
     rest,
     invs,
+    centres,
     left_ops,
     h_wide,
     reach,
@@ -170,11 +171,14 @@
         )
         right_ops[g, :, k * slots : (k + 1) * slots] = right.astype(BF16)
 
-    centres = []
+    def centres_of(g):
+        mid = centres[g]
+        return mid[0:4], mid[4:7]
+
     for g in range(nb):
         mid = centre(g)
         mid_pos = jnp.concatenate([mid[0:3], jnp.zeros((1, 1), F32)], axis=0)
-        centres.append((mid_pos, mid[3:6]))
+        centres[g] = jnp.concatenate([mid_pos, mid[3:6], jnp.zeros((1, 1), F32)], axis=0)
         shifted, length = offset(near[mine + g], mid_pos)
         own = jnp.where(row4 < 3, -2.0 * shifted, length)
         p0, p1, p2 = pieces(jnp.concatenate([own, own], axis=0))
@@ -191,7 +195,7 @@
         )
         left_ops[g] = left.T.astype(BF16)
         build_right(g, 0, mid_pos)
-        h_row = particles[6, g : g + 1, :]
+        h_row = particles[6, pl.ds(g, 1), :]
         h_wide[g] = jnp.broadcast_to(h_row, (slots, slots)).T
         reach[g] = 2.0 * h_wide[g]
         limit[g] = 2.5 * h_wide[g]
@@ -199,8 +203,9 @@
     wait(near, 0, recv_sem)
     send(rest, 1)
 
-    for g in range(nb):
-        mid_pos, mid_vel = centres[g]
+    @pl.loop(0, nb)
+    def density_pass(g):
+        mid_pos, mid_vel = centres_of(g)
         for k in range(1, members):
             build_right(g, k, mid_pos)
         acc = jnp.zeros((slots, slots), F32)
@@ -223,16 +228,17 @@
                 acc += (gap2 * gap2) * ((limit[g] - gap) * mass)
         total = jnp.sum(acc.T, axis=0, keepdims=True)
         filled = filled_of(g)
-        h_row = particles[6, g : g + 1, :]
+        h_row = particles[6, pl.ds(g, 1), :]
         h2 = h_row * h_row
         raw = total * ((weight_norm / 8.0) / (h2 * h2 * h2 * h2))
-        density_out[g : g + 1, :] = filled * raw
+        density_out[pl.ds(g, 1), :] = filled * raw
         invs[mine + g] = 1.0 / (filled * raw + (1.0 - filled))
 
     send(invs, 2)
     wait(rest, 1, recv_sem)
 
-    for g in range(nb):
+    @pl.loop(0, nb)
+    def force_pass(g):
         for k in range(members):
             cols = slice(k * slots, (k + 1) * slots)
             both = h_wide[g] + rest[member_index(g, k)][3:4]
@@ -247,8 +253,9 @@
 
     wait(invs, 2, recv_sem)
 
-    for g in range(nb):
-        mid_pos, mid_vel = centres[g]
+    @pl.loop(0, nb)
+    def sum_pass(g):
+        mid_pos, mid_vel = centres_of(g)
         mid_four = jnp.concatenate([mid_vel, jnp.zeros((1, 1), F32)], axis=0)
         for k in range(members):
             at = member_index(g, k)
@@ -303,6 +310,7 @@
             pltpu.VMEM((bins, 4, slots), F32),
             pltpu.VMEM((bins, 4, slots), F32),
             pltpu.VMEM((bins, 1, slots), F32),
+            pltpu.VMEM((nb, 8, 1), F32),
             pltpu.VMEM((nb, slots, 32), BF16),
             pltpu.VMEM((nb, slots, slots), F32),
             pltpu.VMEM((nb, slots, slots), F32),

time: 17.4 us -> 19.2 us (1.10)
  Pallas kernels: 15.4 us -> 17.1 us
    pallas_call x1, Pallas kernels: 15.4 us -> 17.1 us  [per_device(): pl.pallas_call(functools.partial(kernel, n_slab, n_work), out_shape=(jax....]
where the time goes in v4:
time: 19.2 us; the launch traced here: 18.9 us
  Pallas kernels  17.1 us (89%)
  local copies, waits for them, and re-layouts  1.17 us (6%)
  between operations  0.64 us (3%)
    pallas_call x1, Pallas kernels, per_device(): pl.pallas_call(functools.partial(kernel, n_slab, n_work), out_shape=(jax....  17.1 us
    unnamed x2, local copies, waits for them, and re-layouts  1.17 us

profile of v4, /device:TPU:0, one launch (start us, length us, event | category | flops | bytes accessed | tf_op | source)
XLA Modules:
  0.0 18.9 jit_solution(15323042657882666761)
XLA Ops:
  0.6 17.1 %shard_map.50 = (f32[4,128]{1,0:T(4,128)S(1)}, f32[3,4,128]{2,1,0:T(4,128)S(1)}) custom-call(f32[8,4,128]{2,1,0:T(4,128)} %particles_in.1, s32[4]{0:T(128)} %counts_in.1, s32[4,8]{1,0:T(4,128)} %partners_in.1), custom_call_target="tpu_custom_call" | custom-call | flops 28835840 | bytes 65536 | tf_op jit(solution)/shard_map/pallas_call | solution.py:298
  17.7 0.6 %copy.7 = f32[4,128]{1,0:T(4,128)} copy(f32[4,128]{1,0:T(4,128)S(1)} %get-tuple-element.4) | data formatting | bytes 4096
  18.3 0.6 %copy.8 = f32[3,4,128]{2,1,0:T(4,128)} copy(f32[3,4,128]{2,1,0:T(4,128)S(1)} %get-tuple-element.5) | data formatting | bytes 12288

commit v5 on v3

--- a/solution.py
+++ b/solution.py
@@ -61,6 +61,8 @@
     radius,
     force_hi,
     force_lo,
+    partial,
+    bases,
     sources,
     send_sem,
     recv_sem,
@@ -87,14 +89,21 @@
 
     barrier = pltpu.get_barrier_semaphore()
 
+    def peer(d):
+        if n_work & (n_work - 1):
+            return lax.rem(me + d + 1, n_work)
+        flips, other, bit = n_work - 1 - d, me, 1
+        while bit < n_work:
+            other = other + bit * ((flips // bit) % 2) * (1 - 2 * ((me // bit) % 2))
+            bit *= 2
+        return other
+
     def greet(d):
-        pl.semaphore_signal(
-            barrier, 1, device_id={"work": lax.rem(me + d + 1, n_work)}, device_id_type=MESH
-        )
-
+        pl.semaphore_signal(barrier, 1, device_id={"work": peer(d)}, device_id_type=MESH)
+
+    each(n_work - 1, greet)
     for other in (up, down):
         pl.semaphore_signal(barrier, 1, device_id={"slab": other}, device_id_type=MESH)
-    each(n_work - 1, greet)
 
     lane = lax.broadcasted_iota(jnp.int32, (1, slots), 1)
 
@@ -110,28 +119,29 @@
 
     pl.semaphore_wait(barrier, n_work + 1)
 
-    def send(buf, step):
+    def send(buf, step, slab_step):
         src = buf.at[pl.ds(mine, nb)]
 
-        def start(dst, where):
+        def start(dst, where, arrived):
             pltpu.make_async_remote_copy(
                 src_ref=src,
                 dst_ref=dst,
                 send_sem=send_sem.at[step],
-                recv_sem=recv_sem.at[step],
+                recv_sem=recv_sem.at[arrived],
                 device_id=where,
                 device_id_type=MESH,
             ).start()
 
-        each(n_work - 1, lambda d: start(src, {"work": lax.rem(me + d + 1, n_work)}))
-        start(buf.at[pl.ds(slab_bins, nb)], {"slab": up})
-        start(buf.at[pl.ds(slab_bins + nb, nb)], {"slab": down})
-
-    def wait(buf, step, sem):
-        block = buf.at[pl.ds(0, slab_bins + nb)]
-        pltpu.make_async_copy(block, block, sem.at[step]).wait()
-
-    send(near, 0)
+        start(buf.at[pl.ds(slab_bins, nb)], {"slab": up}, slab_step)
+        start(buf.at[pl.ds(slab_bins + nb, nb)], {"slab": down}, slab_step)
+        each(n_work - 1, lambda d: start(src, {"work": peer(d)}, step))
+
+    def wait(buf, bins, sem):
+        block = buf.at[pl.ds(0, bins)]
+        pltpu.make_async_copy(block, block, sem).wait()
+
+    everyone = slab_bins + nb
+    send(near, 0, 3)
 
     def member_index(g, k):
         if k == 0:
@@ -196,31 +206,35 @@
         reach[g] = 2.0 * h_wide[g]
         limit[g] = 2.5 * h_wide[g]
 
-    wait(near, 0, recv_sem)
-    send(rest, 1)
-
-    for g in range(nb):
-        mid_pos, mid_vel = centres[g]
-        for k in range(1, members):
-            build_right(g, k, mid_pos)
-        acc = jnp.zeros((slots, slots), F32)
-        for k0 in range(0, members, 2):
-            ks = range(k0, min(k0 + 2, members))
-            square = jnp.dot(
-                left_ops[g],
-                right_ops[g, :, k0 * slots : (k0 + len(ks)) * slots],
-                preferred_element_type=F32,
-            )
+    def density_part(g, ks, acc):
+        mid_pos = centres[g][0]
+        for k in ks:
+            if k:
+                build_right(g, k, mid_pos)
+        for k0 in range(ks[0], ks[-1] + 1, 2):
+            pair = [k for k in (k0, k0 + 1) if k in ks]
+            cols = slice(k0 * slots, (k0 + len(pair)) * slots)
+            square = jnp.dot(left_ops[g], right_ops[g, :, cols], preferred_element_type=F32)
             square = jnp.maximum(square, 1e-30)
             dist = square * lax.rsqrt(square)
-            radius[g, :, k0 * slots : (k0 + len(ks)) * slots] = dist
-            for k in ks:
+            radius[g, :, cols] = dist
+            for k in pair:
                 mass = near[member_index(g, k)][3:4]
                 gap = jnp.maximum(
                     reach[g] - dist[:, (k - k0) * slots : (k - k0 + 1) * slots], 0.0
                 )
                 gap2 = gap * gap
                 acc += (gap2 * gap2) * ((limit[g] - gap) * mass)
+        return acc
+
+    wait(near, 2 * nb, recv_sem.at[3])
+    for g in range(nb):
+        partial[g] = density_part(g, range(3), jnp.zeros((slots, slots), F32))
+    wait(near, slab_bins - nb, recv_sem.at[0])
+    send(rest, 1, 1)
+
+    for g in range(nb):
+        acc = density_part(g, range(3, members), partial[g])
         total = jnp.sum(acc.T, axis=0, keepdims=True)
         filled = filled_of(g)
         h_row = particles[6, g : g + 1, :]
@@ -229,8 +243,8 @@
         density_out[g : g + 1, :] = filled * raw
         invs[mine + g] = 1.0 / (filled * raw + (1.0 - filled))
 
-    send(invs, 2)
-    wait(rest, 1, recv_sem)
+    send(invs, 2, 2)
+    wait(rest, everyone, recv_sem.at[1])
 
     for g in range(nb):
         for k in range(members):
@@ -245,8 +259,6 @@
             force_hi[g, :, cols] = high
             force_lo[g, :, cols] = (force - high.astype(F32)).astype(BF16)
 
-    wait(invs, 2, recv_sem)
-
     for g in range(nb):
         mid_pos, mid_vel = centres[g]
         mid_four = jnp.concatenate([mid_vel, jnp.zeros((1, 1), F32)], axis=0)
@@ -255,20 +267,34 @@
             place = near[at]
             mass = place[3:4]
             moment = jnp.where(row4 < 3, place - mid_pos, 1.0) * mass
-            speed = (rest[at] - mid_four) * mass
-            inv = invs[at]
-            first = jnp.concatenate([moment, moment * inv], axis=0)
-            second = jnp.where(row8 < 3, jnp.concatenate([speed, speed], axis=0) * inv, 0.0)
-            b0, b1, b2 = pieces(jnp.concatenate([first, second], axis=0))
-            sources[g, :, k * slots : (k + 1) * slots] = jnp.concatenate(
-                [b0, b1, b2], axis=0
-            ).astype(BF16)
+            speed = jnp.where(row4 < 3, rest[at] - mid_four, 0.0) * mass
+            cols = slice(k * slots, (k + 1) * slots)
+            bases[g, 0:8, cols] = jnp.concatenate([moment, moment], axis=0)
+            bases[g, 8:16, cols] = jnp.concatenate([speed, speed], axis=0)
+
+    wait(invs, everyone, recv_sem.at[2])
+
+    for g in range(nb):
+        mid_pos, mid_vel = centres[g]
+        for k in range(members):
+            cols = slice(k * slots, (k + 1) * slots)
+            inv = invs[member_index(g, k)]
+            source = jnp.concatenate(
+                [
+                    bases[g, 0:8, cols] * jnp.where(row8 < 4, 1.0, inv),
+                    bases[g, 8:16, cols] * inv,
+                ],
+                axis=0,
+            )
+            first = source.astype(BF16)
+            sources[g, 0:16, cols] = first
+            sources[g, 16:32, cols] = (source - first.astype(F32)).astype(BF16)
         dims = (((1,), (1,)), ((), ()))
         sums = lax.dot_general(
             force_hi[g], sources[g], dims, preferred_element_type=F32
         ) + lax.dot_general(force_lo[g], sources[g], dims, preferred_element_type=F32)
         sums = sums.T
-        sums = sums[0:16] + sums[16:32] + sums[32:48]
+        sums = sums[0:16] + sums[16:32]
         own = particles[:, g, :]
         pos = own[0:3] - mid_pos[0:3]
         vel = own[3:6] - mid_vel
@@ -278,7 +304,7 @@
         accel_out[:, g, :] = result * (filled_of(g) * (32.0 * force_norm))
 
     for step, buf in enumerate((near, rest, invs)):
-        wait(buf, step, send_sem)
+        wait(buf, everyone, send_sem.at[step])
 
 
 def per_device(n_slab, n_work, particles, counts, partners):
@@ -311,9 +337,11 @@
             pltpu.VMEM((nb, slots, members * slots), F32),
             pltpu.VMEM((nb, slots, members * slots), BF16),
             pltpu.VMEM((nb, slots, members * slots), BF16),
-            pltpu.VMEM((nb, 48, members * slots), BF16),
+            pltpu.VMEM((nb, slots, slots), F32),
+            pltpu.VMEM((nb, 16, members * slots), F32),
+            pltpu.VMEM((nb, 32, members * slots), BF16),
             pltpu.SemaphoreType.DMA((3,)),
-            pltpu.SemaphoreType.DMA((3,)),
+            pltpu.SemaphoreType.DMA((4,)),
             pltpu.SemaphoreType.DMA((3,)),
         ],
         compiler_params=pltpu.CompilerParams(

time: 17.4 us -> 16.9 us (0.971)
  Pallas kernels: 15.4 us -> 14.9 us
    pallas_call x1, Pallas kernels: 15.4 us -> 14.9 us  [per_device(): pl.pallas_call(functools.partial(kernel, n_slab, n_work), out_shape=(jax....]
where the time goes in v5:
time: 16.9 us; the launch traced here: 16.7 us
  Pallas kernels  14.9 us (88%)
  local copies, waits for them, and re-layouts  1.17 us (7%)
  between operations  0.64 us (4%)
    pallas_call x1, Pallas kernels, per_device(): pl.pallas_call(functools.partial(kernel, n_slab, n_work), out_shape=(jax....  14.9 us
    unnamed x2, local copies, waits for them, and re-layouts  1.17 us

profile of v5, /device:TPU:0, one launch (start us, length us, event | category | flops | bytes accessed | tf_op | source)
XLA Modules:
  0.0 16.7 jit_solution(13494485461935010912)
XLA Ops:
  0.6 14.9 %shard_map.50 = (f32[4,128]{1,0:T(4,128)S(1)}, f32[3,4,128]{2,1,0:T(4,128)S(1)}) custom-call(f32[8,4,128]{2,1,0:T(4,128)} %particles_in.1, s32[4]{0:T(128)} %counts_in.1, s32[4,8]{1,0:T(4,128)} %partners_in.1), custom_call_target="tpu_custom_call" | custom-call | flops 28835840 | bytes 65536 | tf_op jit(solution)/shard_map/pallas_call | solution.py:317
  15.5 0.6 %copy.7 = f32[4,128]{1,0:T(4,128)} copy(f32[4,128]{1,0:T(4,128)S(1)} %get-tuple-element.4) | data formatting | bytes 4096
  16.1 0.6 %copy.8 = f32[3,4,128]{2,1,0:T(4,128)} copy(f32[3,4,128]{2,1,0:T(4,128)S(1)} %get-tuple-element.5) | data formatting | bytes 12288

commit v6 on v5

--- a/solution.py
+++ b/solution.py
@@ -227,27 +227,8 @@
                 acc += (gap2 * gap2) * ((limit[g] - gap) * mass)
         return acc
 
-    wait(near, 2 * nb, recv_sem.at[3])
-    for g in range(nb):
-        partial[g] = density_part(g, range(3), jnp.zeros((slots, slots), F32))
-    wait(near, slab_bins - nb, recv_sem.at[0])
-    send(rest, 1, 1)
-
-    for g in range(nb):
-        acc = density_part(g, range(3, members), partial[g])
-        total = jnp.sum(acc.T, axis=0, keepdims=True)
-        filled = filled_of(g)
-        h_row = particles[6, g : g + 1, :]
-        h2 = h_row * h_row
-        raw = total * ((weight_norm / 8.0) / (h2 * h2 * h2 * h2))
-        density_out[g : g + 1, :] = filled * raw
-        invs[mine + g] = 1.0 / (filled * raw + (1.0 - filled))
-
-    send(invs, 2, 2)
-    wait(rest, everyone, recv_sem.at[1])
-
-    for g in range(nb):
-        for k in range(members):
+    def force_part(g, ks):
+        for k in ks:
             cols = slice(k * slots, (k + 1) * slots)
             both = h_wide[g] + rest[member_index(g, k)][3:4]
             inv = pltpu.reciprocal(both, approx=True)
@@ -258,6 +239,31 @@
             high = force.astype(BF16)
             force_hi[g, :, cols] = high
             force_lo[g, :, cols] = (force - high.astype(F32)).astype(BF16)
+
+    for g in range(nb):
+        partial[g] = density_part(g, range(1), jnp.zeros((slots, slots), F32))
+        force_part(g, range(1))
+    wait(near, 2 * nb, recv_sem.at[3])
+    for g in range(nb):
+        partial[g] = density_part(g, range(1, 3), partial[g])
+    wait(near, slab_bins - nb, recv_sem.at[0])
+    send(rest, 1, 1)
+
+    for g in range(nb):
+        acc = density_part(g, range(3, members), partial[g])
+        total = jnp.sum(acc.T, axis=0, keepdims=True)
+        filled = filled_of(g)
+        h_row = particles[6, g : g + 1, :]
+        h2 = h_row * h_row
+        raw = total * ((weight_norm / 8.0) / (h2 * h2 * h2 * h2))
+        density_out[g : g + 1, :] = filled * raw
+        invs[mine + g] = 1.0 / (filled * raw + (1.0 - filled))
+
+    send(invs, 2, 2)
+    wait(rest, everyone, recv_sem.at[1])
+
+    for g in range(nb):
+        force_part(g, range(1, members))
 
     for g in range(nb):
         mid_pos, mid_vel = centres[g]
@@ -307,6 +313,17 @@
         wait(buf, everyone, send_sem.at[step])
 
 
+def write_out(density, accel, density_out, accel_out, sem):
+    copies = [
+        pltpu.make_async_copy(src, dst, sem.at[i])
+        for i, (src, dst) in enumerate(((density, density_out), (accel, accel_out)))
+    ]
+    for copy in copies:
+        copy.start()
+    for copy in copies:
+        copy.wait()
+
+
 def per_device(n_slab, n_work, particles, counts, partners):
     channels, nb, slots = particles.shape
     members = 3 + partners.shape[1]
@@ -314,12 +331,13 @@
     vmem = pl.BlockSpec(memory_space=pltpu.VMEM)
     hbm = pl.BlockSpec(memory_space=pltpu.HBM)
     pairs = nb * members * slots * slots
-    return pl.pallas_call(
+    results = (
+        jax.ShapeDtypeStruct((nb, slots), F32),
+        jax.ShapeDtypeStruct((3, nb, slots), F32),
+    )
+    computed = pl.pallas_call(
         functools.partial(kernel, n_slab, n_work),
-        out_shape=(
-            jax.ShapeDtypeStruct((nb, slots), F32),
-            jax.ShapeDtypeStruct((3, nb, slots), F32),
-        ),
+        out_shape=results,
         in_specs=[hbm, hbm, hbm],
         out_specs=(vmem, vmem),
         scratch_shapes=[
@@ -349,6 +367,13 @@
         ),
         cost_estimate=pl.CostEstimate(flops=40 * pairs, bytes_accessed=65536, transcendentals=0),
     )(*(pltpu.with_memory_space_constraint(a, pltpu.HBM) for a in (particles, counts, partners)))
+    return pl.pallas_call(
+        write_out,
+        out_shape=results,
+        in_specs=[vmem, vmem],
+        out_specs=(hbm, hbm),
+        scratch_shapes=[pltpu.SemaphoreType.DMA((2,))],
+    )(*computed)
 
 
 def solution(mesh):

time: 16.9 us -> 18.1 us (1.071)
  Pallas kernels: 14.9 us -> 16 us
    pallas_call x1 -> x2, Pallas kernels: 14.9 us -> 16 us  [the longest x1 14.7 us: per_device(): pl.pallas_call(functools.partial(kernel, n_slab, n_work), out_shape=resul...]
    unnamed x2 -> x4, local copies, waits for them, and re-layouts: 1.17 us -> 1.15 us
where the time goes in v6:
time: 18.1 us; the launch traced here: 17.8 us
  Pallas kernels  16 us (88%)
  local copies, waits for them, and re-layouts  1.15 us (6%)
  between operations  0.65 us (4%)
    pallas_call x1, Pallas kernels, per_device(): pl.pallas_call(functools.partial(kernel, n_slab, n_work), out_shape=resul...  14.7 us
    pallas_call x1, Pallas kernels, per_device(): pl.pallas_call(write_out, out_shape=results, in_specs=[vmem, vmem], out_s...  1.31 us
    unnamed x4, local copies, waits for them, and re-layouts  1.15 us

profile of v6, /device:TPU:0, one launch (start us, length us, event | category | flops | bytes accessed | tf_op | source)
XLA Modules:
  0.0 17.8 jit_solution(8586405388870869599)
XLA Ops:
  0.6 14.7 %shard_map.50 = (f32[4,128]{1,0:T(4,128)S(1)}, f32[3,4,128]{2,1,0:T(4,128)S(1)}) custom-call(f32[8,4,128]{2,1,0:T(4,128)} %particles_in.1, s32[4]{0:T(128)} %counts_in.1, s32[4,8]{1,0:T(4,128)} %partners_in.1), custom_call_target="tpu_custom_call" | custom-call | flops 28835840 | bytes 65536 | tf_op jit(solution)/shard_map/pallas_call | solution.py:338
  15.3 0.0 copy-start
  15.3 0.6 %copy-done = f32[3,4,128]{2,1,0:T(4,128)} copy-done((f32[3,4,128]{2,1,0:T(4,128)}, f32[3,4,128]{2,1,0:T(4,128)S(1)}, u32[]{:S(2)}) %copy-start) | copy-done | bytes 6168
  15.9 0.0 copy-start.1
  15.9 0.6 %copy-done.1 = f32[4,128]{1,0:T(4,128)} copy-done((f32[4,128]{1,0:T(4,128)}, f32[4,128]{1,0:T(4,128)S(1)}, u32[]{:S(2)}) %copy-start.1) | copy-done | bytes 2072
  16.5 1.3 %shard_map.51 = (f32[4,128]{1,0:T(4,128)}, f32[3,4,128]{2,1,0:T(4,128)}) custom-call(f32[4,128]{1,0:T(4,128)} %copy-done.1, f32[3,4,128]{2,1,0:T(4,128)} %copy-done), custom_call_target="tpu_custom_call" | custom-call | tf_op jit(solution)/shard_map/pallas_call | solution.py:370
Async XLA Ops:
  15.3 0.6 %copy-start = (f32[3,4,128]{2,1,0:T(4,128)}, f32[3,4,128]{2,1,0:T(4,128)S(1)}, u32[]{:S(2)}) copy-start(f32[3,4,128]{2,1,0:T(4,128)S(1)} %get-tuple-element.5.accel) | copy-start | bytes 18436
  15.9 0.6 %copy-start.1 = (f32[4,128]{1,0:T(4,128)}, f32[4,128]{1,0:T(4,128)S(1)}, u32[]{:S(2)}) copy-start(f32[4,128]{1,0:T(4,128)S(1)} %get-tuple-element.4.density) | copy-start | bytes 6148

commit v7 on v6

--- a/solution.py
+++ b/solution.py
@@ -373,7 +373,8 @@
         in_specs=[vmem, vmem],
         out_specs=(hbm, hbm),
         scratch_shapes=[pltpu.SemaphoreType.DMA((2,))],
-    )(*computed)
+        compiler_params=pltpu.CompilerParams(vmem_limit_bytes=1024 * 1024),
+    )(*(pltpu.with_memory_space_constraint(a, pltpu.VMEM) for a in computed))
 
 
 def solution(mesh):

time: 18.1 us -> 16.2 us (0.90)
  local copies, waits for them, and re-layouts: 1.15 us -> 0 us
  Pallas kernels: 16 us -> 15.3 us
    unnamed x4 -> x0, local copies, waits for them, and re-layouts: 1.15 us -> none
    pallas_call x1, Pallas kernels: 1.31 us -> 0.62 us  [per_device(): pl.pallas_call(write_out, out_shape=results, in_specs=[vmem, vmem], out_s...]
where the time goes in v7:
time: 16.2 us; the launch traced here: 15.9 us
  Pallas kernels  15.3 us (94%)
  between operations  0.64 us (4%)
    pallas_call x1, Pallas kernels, per_device(): pl.pallas_call(functools.partial(kernel, n_slab, n_work), out_shape=resul...  14.7 us
    pallas_call x1, Pallas kernels, per_device(): pl.pallas_call(write_out, out_shape=results, in_specs=[vmem, vmem], out_s...  0.62 us

profile of v7, /device:TPU:0, one launch (start us, length us, event | category | flops | bytes accessed | tf_op | source)
XLA Modules:
  0.0 15.9 jit_solution(5999877962439234974)
XLA Ops:
  0.6 14.7 %shard_map.50 = (f32[4,128]{1,0:T(4,128)S(1)}, f32[3,4,128]{2,1,0:T(4,128)S(1)}) custom-call(f32[8,4,128]{2,1,0:T(4,128)} %particles_in.1, s32[4]{0:T(128)} %counts_in.1, s32[4,8]{1,0:T(4,128)} %partners_in.1), custom_call_target="tpu_custom_call" | custom-call | flops 28835840 | bytes 65536 | tf_op jit(solution)/shard_map/pallas_call | solution.py:338
  15.3 0.6 %shard_map.51 = (f32[4,128]{1,0:T(4,128)}, f32[3,4,128]{2,1,0:T(4,128)}) custom-call(f32[4,128]{1,0:T(4,128)S(1)} %get-tuple-element.4.density, f32[3,4,128]{2,1,0:T(4,128)S(1)} %get-tuple-element.5.accel), custom_call_target="tpu_custom_call" | custom-call | tf_op jit(solution)/shard_map/pallas_call | solution.py:370

commit v8 on v7

--- a/solution.py
+++ b/solution.py
@@ -244,10 +244,10 @@
         partial[g] = density_part(g, range(1), jnp.zeros((slots, slots), F32))
         force_part(g, range(1))
     wait(near, 2 * nb, recv_sem.at[3])
+    send(rest, 1, 1)
     for g in range(nb):
         partial[g] = density_part(g, range(1, 3), partial[g])
     wait(near, slab_bins - nb, recv_sem.at[0])
-    send(rest, 1, 1)
 
     for g in range(nb):
         acc = density_part(g, range(3, members), partial[g])

time: 16.2 us -> 16.1 us (level)
  no operation moved by 1% of the time
where the time goes in v8:
time: 16.1 us; the launch traced here: 15.9 us
  Pallas kernels  15.3 us (95%)
  between operations  0.64 us (4%)
    pallas_call x1, Pallas kernels, per_device(): pl.pallas_call(functools.partial(kernel, n_slab, n_work), out_shape=resul...  14.6 us
    pallas_call x1, Pallas kernels, per_device(): pl.pallas_call(write_out, out_shape=results, in_specs=[vmem, vmem], out_s...  0.62 us

profile of v8, /device:TPU:0, one launch (start us, length us, event | category | flops | bytes accessed | tf_op | source)
XLA Modules:
  0.0 15.9 jit_solution(4773488498443592661)
XLA Ops:
  0.6 14.6 %shard_map.50 = (f32[4,128]{1,0:T(4,128)S(1)}, f32[3,4,128]{2,1,0:T(4,128)S(1)}) custom-call(f32[8,4,128]{2,1,0:T(4,128)} %particles_in.1, s32[4]{0:T(128)} %counts_in.1, s32[4,8]{1,0:T(4,128)} %partners_in.1), custom_call_target="tpu_custom_call" | custom-call | flops 28835840 | bytes 65536 | tf_op jit(solution)/shard_map/pallas_call | solution.py:338
  15.3 0.6 %shard_map.51 = (f32[4,128]{1,0:T(4,128)}, f32[3,4,128]{2,1,0:T(4,128)}) custom-call(f32[4,128]{1,0:T(4,128)S(1)} %get-tuple-element.4.density, f32[3,4,128]{2,1,0:T(4,128)S(1)} %get-tuple-element.5.accel), custom_call_target="tpu_custom_call" | custom-call | tf_op jit(solution)/shard_map/pallas_call | solution.py:370

commit v9 on v8

--- a/solution.py
+++ b/solution.py
@@ -259,7 +259,7 @@
         density_out[g : g + 1, :] = filled * raw
         invs[mine + g] = 1.0 / (filled * raw + (1.0 - filled))
 
-    send(invs, 2, 2)
+    send(invs, 2, 4)
     wait(rest, everyone, recv_sem.at[1])
 
     for g in range(nb):
@@ -278,11 +278,8 @@
             bases[g, 0:8, cols] = jnp.concatenate([moment, moment], axis=0)
             bases[g, 8:16, cols] = jnp.concatenate([speed, speed], axis=0)
 
-    wait(invs, everyone, recv_sem.at[2])
-
-    for g in range(nb):
-        mid_pos, mid_vel = centres[g]
-        for k in range(members):
+    def source_part(g, ks):
+        for k in ks:
             cols = slice(k * slots, (k + 1) * slots)
             inv = invs[member_index(g, k)]
             source = jnp.concatenate(
@@ -295,6 +292,17 @@
             first = source.astype(BF16)
             sources[g, 0:16, cols] = first
             sources[g, 16:32, cols] = (source - first.astype(F32)).astype(BF16)
+
+    for g in range(nb):
+        source_part(g, range(1))
+    wait(invs, 2 * nb, recv_sem.at[4])
+    for g in range(nb):
+        source_part(g, range(1, 3))
+    wait(invs, slab_bins - nb, recv_sem.at[2])
+
+    for g in range(nb):
+        mid_pos, mid_vel = centres[g]
+        source_part(g, range(3, members))
         dims = (((1,), (1,)), ((), ()))
         sums = lax.dot_general(
             force_hi[g], sources[g], dims, preferred_element_type=F32
@@ -359,7 +367,7 @@
             pltpu.VMEM((nb, 16, members * slots), F32),
             pltpu.VMEM((nb, 32, members * slots), BF16),
             pltpu.SemaphoreType.DMA((3,)),
-            pltpu.SemaphoreType.DMA((4,)),
+            pltpu.SemaphoreType.DMA((5,)),
             pltpu.SemaphoreType.DMA((3,)),
         ],
         compiler_params=pltpu.CompilerParams(

time: 16.1 us -> 16.1 us (level)
  no operation moved by 1% of the time
where the time goes in v9:
time: 16.1 us; the launch traced here: 15.9 us
  Pallas kernels  15.2 us (94%)
  between operations  0.64 us (4%)
    pallas_call x1, Pallas kernels, per_device(): pl.pallas_call(functools.partial(kernel, n_slab, n_work), out_shape=resul...  14.6 us
    pallas_call x1, Pallas kernels, per_device(): pl.pallas_call(write_out, out_shape=results, in_specs=[vmem, vmem], out_s...  0.62 us

profile of v9, /device:TPU:0, one launch (start us, length us, event | category | flops | bytes accessed | tf_op | source)
XLA Modules:
  0.0 15.9 jit_solution(1744775255207221481)
XLA Ops:
  0.6 14.6 %shard_map.50 = (f32[4,128]{1,0:T(4,128)S(1)}, f32[3,4,128]{2,1,0:T(4,128)S(1)}) custom-call(f32[8,4,128]{2,1,0:T(4,128)} %particles_in.1, s32[4]{0:T(128)} %counts_in.1, s32[4,8]{1,0:T(4,128)} %partners_in.1), custom_call_target="tpu_custom_call" | custom-call | flops 28835840 | bytes 65536 | tf_op jit(solution)/shard_map/pallas_call | solution.py:346
  15.3 0.6 %shard_map.51 = (f32[4,128]{1,0:T(4,128)}, f32[3,4,128]{2,1,0:T(4,128)}) custom-call(f32[4,128]{1,0:T(4,128)S(1)} %get-tuple-element.4.density, f32[3,4,128]{2,1,0:T(4,128)S(1)} %get-tuple-element.5.accel), custom_call_target="tpu_custom_call" | custom-call | tf_op jit(solution)/shard_map/pallas_call | solution.py:378
